TPU v7x, 32 devices: a whole 2x2x4 slice. The times are simulated.
32 devices in a mesh: wide: 8 (over y, x, core), blk: 4 (over z).
Axes of the slice: x: 2, y: 2, z: 4, core: 2. Of those that a mesh axis runs over, the one named last changes fastest.
Arguments:
- features: bfloat16 [512, 768], P('blk'), may hold values from -6 to 6
- weights: bfloat16 [32768, 768], P(('wide', 'blk')), may hold values from -0.21875 to 0.21875
- momentum: bfloat16 [32768, 768], P(('wide', 'blk')), may hold values from -48 to 48
- targets: bfloat16 [512, 32768], P(None, ('wide', 'blk')), may hold values from 0 to 1
Outputs:
- new_weights: bfloat16 [32768, 768], P(('wide', 'blk'))
- new_momentum: bfloat16 [32768, 768], P(('wide', 'blk'))
- feature_grad: bfloat16 [512, 768], P('blk', 'wide')
All inputs are finite; a program needn't handle non-finite values.
Results may differ from a plain program's by a relative error of at most 0.009.
Values may be sent and summed in bfloat16 or wider, within the bound.
A program may use at most 64 MiB of HBM per device.

v0:
```python
import jax
import jax.numpy as jnp
from jax import lax
from jax.sharding import PartitionSpec as P


def shifted(block, axis, distance):
    devices = range(lax.axis_size(axis))
    route = [((i - distance) % len(devices), i) for i in devices]
    return lax.ppermute(block, axis, route)


def shards(features, weights, momentum, targets):
    cycle_size = lax.axis_size("blk")
    cycle_place = lax.axis_index("blk")
    row_count = features.shape[0]
    width = features.shape[1]

    def errors_of(row_block, target_rows):
        scores = lax.dot_general(
            row_block, weights, (((1,), (1,)), ((), ())), preferred_element_type=jnp.float32
        )
        return (jax.nn.sigmoid(scores) - target_rows.astype(jnp.float32)).astype(jnp.bfloat16)

    def weight_part(error_rows, row_block):
        return lax.dot_general(
            error_rows, row_block, (((0,), (0,)), ((), ())), preferred_element_type=jnp.float32
        )

    def back_part(error_rows):
        return jnp.dot(error_rows, weights, preferred_element_type=jnp.float32)

    grad_start = jnp.zeros(weights.shape, jnp.float32)

    def turn(turn_index, state_now):
        row_block, moving, weight_grad, spread = state_now
        first_row = (cycle_place - turn_index) % cycle_size * row_count
        error_rows = errors_of(
            row_block, lax.dynamic_slice_in_dim(targets, first_row, row_count, 0)
        )
        weight_grad = weight_grad + weight_part(error_rows, row_block)
        term_rows = back_part(error_rows)
        row_block = shifted(row_block, "blk", 1)
        moving = shifted(moving + term_rows, "blk", 1)
        return (row_block, moving, weight_grad, spread)

    moving_start = jnp.zeros((row_count, width), jnp.float32)
    spread_start = jnp.zeros((1, width), jnp.float32)
    final_state = lax.fori_loop(
        0, cycle_size, turn, (features, moving_start, grad_start, spread_start)
    )
    moving, weight_grad, spread = (final_state[1], final_state[2], final_state[3])
    feature_grad = lax.psum_scatter(moving, "wide", scatter_dimension=1, tiled=True).astype(
        jnp.bfloat16
    )
    new_momentum = (0.9 * momentum.astype(jnp.float32) + weight_grad).astype(jnp.bfloat16)
    new_weights = (weights.astype(jnp.float32) - 0.002 * new_momentum.astype(jnp.float32)).astype(
        jnp.bfloat16
    )
    return (new_weights, new_momentum, feature_grad)


def solution(mesh):
    placed = (
        P("blk", None),
        P(("wide", "blk"), None),
        P(("wide", "blk"), None),
        P(None, ("wide", "blk")),
    )
    return jax.shard_map(
        shards,
        mesh=mesh,
        in_specs=placed,
        out_specs=(P(("wide", "blk"), None), P(("wide", "blk"), None), P("blk", "wide")),
        check_vma=False,
    )
```

profile of v0, /device:TPU:0, one launch (start us, length us, event | category | flops | bytes accessed | tf_op | source)
XLA Modules:
  0.0 127.5 jit_solution(5479861713671745770)
XLA Ops:
  7.2 0.0 reduce-scatter.2.cloned.1.call-start
  7.2 1.6 %copy.21 = bf16[128,768]{1,0:T(8,128)(2,1)} copy(bf16[128,768]{1,0:T(8,128)(2,1)} %param.6) | data formatting | bytes 393216
  8.8 0.8 broadcast_in_dim.6
  9.6 75.2 %while.20 = (s32[]{:T(128)}, bf16[128,768]{1,0:T(8,128)(2,1)}, f32[128,768]{1,0:T(8,128)}, f32[1024,768]{1,0:T(8,128)S(1)}, bf16[1024,768]{1,0:T(8,128)(2,1)}, /...) while((s32[]{:T(128)}, bf16[128,768]{1,0:T(8,128)(2,1)}, ...), condition=%wide.region_1.2_spmd.clone, body=%wide.region_0.1_spmd.clone.sunk | while | flops 606437376 | bytes 20709788 | solution.py:49
  9.6 1.6 %copy.13 = bf16[128,768]{1,0:T(8,128)(2,1)} copy(bf16[128,768]{1,0:T(8,128)(2,1)} %get-tuple-element.280) | data formatting | bytes 393216 | tf_op jit(solution)/shard_map/while
  11.2 3.0 %collective-permute-start = (bf16[128,768]{1,0:T(8,128)(2,1)}, bf16[128,768]{1,0:T(8,128)(2,1)}, u32[]{:S(2)}, u32[]{:S(2)}) collective-permute-start(bf16[128,768]{1,0:T(8,128)(2,1)} %copy.13), channel_id=1, source_target_pairs={{3,0},{0,1},{1,2},{2,3},{7,4},{4,5},{5,6},{6,7},{11,8},{8,9},{9,10... | collective-permute-start | bytes 589832 | tf_op jit(solution)/shard_map/while/body/eval_jaxpr/ppermute | solution.py:10
  14.2 0.0 copy-start
  14.2 2.3 %fusion.24 = bf16[128,1024]{1,0:T(8,128)(2,1)S(1)} fusion(bf16[128,768]{1,0:T(8,128)(2,1)} %copy.13, bf16[1024,768]{1,0:T(8,128)(2,1)} %get-tuple-element.296, bf16[512,1024]{1,0:T(8,128)(2,1)} %get-tuple-element.298, s32[]{:T(128)S(6)} %select_n.35), kind=kOutput, calls=%fused_computation.6.clone.1 | convolution fusion | flops 202113024 | bytes 2293764 | tf_op jit(solution)/shard_map/while/body/eval_jaxpr/dot_general | solution.py:20
  16.5 0.0 copy-done
  16.5 2.1 %convolution_add_fusion.2 = f32[128,768]{1,0:T(8,128)} fusion(f32[128,768]{1,0:T(8,128)} %get-tuple-element.281, bf16[128,1024]{1,0:T(8,128)(2,1)S(1)} %fusion.24, bf16[1024,768]{1,0:T(8,128)(2,1)S(1)} %copy-done), kind=kOutput, calls=%fused_computation.7.clone.1 | convolution fusion | flops 201424896 | bytes 2621440 | tf_op jit(solution)/shard_map/while/body/eval_jaxpr/dot_general | solution.py:31
  18.7 1.6 %collective-permute-start.1 = (f32[128,768]{1,0:T(8,128)}, f32[128,768]{1,0:T(8,128)}, u32[]{:S(2)}, u32[]{:S(2)}) collective-permute-start(f32[128,768]{1,0:T(8,128)} %convolution_add_fusion.2), channel_id=1, source_target_pairs={{3,0},{0,1},{1,2},{2,3},{7,4},{4,5},{5,6},{6,7},{11,8},{8,9},{9,10... | collective-permute-start | bytes 1179656 | tf_op jit(solution)/shard_map/while/body/eval_jaxpr/ppermute | solution.py:10
  20.2 2.0 %select_add_fusion.2 = f32[1024,768]{1,0:T(8,128)S(1)} fusion(f32[1024,768]{1,0:T(8,128)S(1)} %get-tuple-element.282, bf16[128,1024]{1,0:T(8,128)(2,1)S(1)} %fusion.24, bf16[128,768]{1,0:T(8,128)(2,1)} %copy.13, pred[]{:T(512)S(6)} %compare.4), kind=kOutput, calls=%fused_computation.clone.1 | convolution fusion | flops 202899456 | bytes 6750209 | tf_op jit(solution)/shard_map/while/body/eval_jaxpr/dot_general | solution.py:26
  22.3 0.0 collective-permute-done
  22.3 9.0 %collective-permute-done.1 = f32[128,768]{1,0:T(8,128)} collective-permute-done((f32[128,768]{1,0:T(8,128)}, f32[128,768]{1,0:T(8,128)}, u32[]{:S(2)}, u32[]{:S(2)}) %collective-permute-start.1) | collective-permute-done | bytes 393248 | tf_op jit(solution)/shard_map/while/body/eval_jaxpr/ppermute | solution.py:10
  31.4 1.6 %copy.13 = bf16[128,768]{1,0:T(8,128)(2,1)} copy(bf16[128,768]{1,0:T(8,128)(2,1)} %get-tuple-element.280) | data formatting | bytes 393216 | tf_op jit(solution)/shard_map/while
  33.0 0.0 collective-permute-start
  33.0 0.0 copy-start
  33.0 2.3 %fusion.24 = bf16[128,1024]{1,0:T(8,128)(2,1)S(1)} fusion(bf16[128,768]{1,0:T(8,128)(2,1)} %copy.13, bf16[1024,768]{1,0:T(8,128)(2,1)} %get-tuple-element.296, bf16[512,1024]{1,0:T(8,128)(2,1)} %get-tuple-element.298, s32[]{:T(128)S(6)} %select_n.35), kind=kOutput, calls=%fused_computation.6.clone.1 | convolution fusion | flops 202113024 | bytes 2293764 | tf_op jit(solution)/shard_map/while/body/eval_jaxpr/dot_general | solution.py:20
  35.3 0.0 copy-done
  35.3 2.1 %convolution_add_fusion.2 = f32[128,768]{1,0:T(8,128)} fusion(f32[128,768]{1,0:T(8,128)} %get-tuple-element.281, bf16[128,1024]{1,0:T(8,128)(2,1)S(1)} %fusion.24, bf16[1024,768]{1,0:T(8,128)(2,1)S(1)} %copy-done), kind=kOutput, calls=%fused_computation.7.clone.1 | convolution fusion | flops 201424896 | bytes 2621440 | tf_op jit(solution)/shard_map/while/body/eval_jaxpr/dot_general | solution.py:31
  37.4 1.3 %collective-permute-start.1 = (f32[128,768]{1,0:T(8,128)}, f32[128,768]{1,0:T(8,128)}, u32[]{:S(2)}, u32[]{:S(2)}) collective-permute-start(f32[128,768]{1,0:T(8,128)} %convolution_add_fusion.2), channel_id=1, source_target_pairs={{3,0},{0,1},{1,2},{2,3},{7,4},{4,5},{5,6},{6,7},{11,8},{8,9},{9,10... | collective-permute-start | bytes 1179656 | tf_op jit(solution)/shard_map/while/body/eval_jaxpr/ppermute | solution.py:10
  38.8 2.0 %select_add_fusion.2 = f32[1024,768]{1,0:T(8,128)S(1)} fusion(f32[1024,768]{1,0:T(8,128)S(1)} %get-tuple-element.282, bf16[128,1024]{1,0:T(8,128)(2,1)S(1)} %fusion.24, bf16[128,768]{1,0:T(8,128)(2,1)} %copy.13, pred[]{:T(512)S(6)} %compare.4), kind=kOutput, calls=%fused_computation.clone.1 | convolution fusion | flops 202899456 | bytes 6750209 | tf_op jit(solution)/shard_map/while/body/eval_jaxpr/dot_general | solution.py:26
  40.8 0.0 collective-permute-done
  40.8 8.4 %collective-permute-done.1 = f32[128,768]{1,0:T(8,128)} collective-permute-done((f32[128,768]{1,0:T(8,128)}, f32[128,768]{1,0:T(8,128)}, u32[]{:S(2)}, u32[]{:S(2)}) %collective-permute-start.1) | collective-permute-done | bytes 393248 | tf_op jit(solution)/shard_map/while/body/eval_jaxpr/ppermute | solution.py:10
  49.2 1.6 %copy.13 = bf16[128,768]{1,0:T(8,128)(2,1)} copy(bf16[128,768]{1,0:T(8,128)(2,1)} %get-tuple-element.280) | data formatting | bytes 393216 | tf_op jit(solution)/shard_map/while
  50.8 0.0 collective-permute-start
  50.8 2.3 %fusion.24 = bf16[128,1024]{1,0:T(8,128)(2,1)S(1)} fusion(bf16[128,768]{1,0:T(8,128)(2,1)} %copy.13, bf16[1024,768]{1,0:T(8,128)(2,1)} %get-tuple-element.296, bf16[512,1024]{1,0:T(8,128)(2,1)} %get-tuple-element.298, s32[]{:T(128)S(6)} %select_n.35), kind=kOutput, calls=%fused_computation.6.clone.1 | convolution fusion | flops 202113024 | bytes 2293764 | tf_op jit(solution)/shard_map/while/body/eval_jaxpr/dot_general | solution.py:20
  53.1 0.0 copy-done
  53.1 2.1 %convolution_add_fusion.2 = f32[128,768]{1,0:T(8,128)} fusion(f32[128,768]{1,0:T(8,128)} %get-tuple-element.281, bf16[128,1024]{1,0:T(8,128)(2,1)S(1)} %fusion.24, bf16[1024,768]{1,0:T(8,128)(2,1)S(1)} %copy-done), kind=kOutput, calls=%fused_computation.7.clone.1 | convolution fusion | flops 201424896 | bytes 2621440 | tf_op jit(solution)/shard_map/while/body/eval_jaxpr/dot_general | solution.py:31
  55.2 0.4 collective-permute-start.1
  55.6 2.0 %select_add_fusion.2 = f32[1024,768]{1,0:T(8,128)S(1)} fusion(f32[1024,768]{1,0:T(8,128)S(1)} %get-tuple-element.282, bf16[128,1024]{1,0:T(8,128)(2,1)S(1)} %fusion.24, bf16[128,768]{1,0:T(8,128)(2,1)} %copy.13, pred[]{:T(512)S(6)} %compare.4), kind=kOutput, calls=%fused_computation.clone.1 | convolution fusion | flops 202899456 | bytes 6750209 | tf_op jit(solution)/shard_map/while/body/eval_jaxpr/dot_general | solution.py:26
  57.7 1.8 %collective-permute-done = bf16[128,768]{1,0:T(8,128)(2,1)} collective-permute-done((bf16[128,768]{1,0:T(8,128)(2,1)}, bf16[128,768]{1,0:T(8,128)(2,1)}, u32[]{:S(2)}, u32[]{:S(2)}) %collective-permute-start) | collective-permute-done | bytes 196640 | tf_op jit(solution)/shard_map/while/body/eval_jaxpr/ppermute | solution.py:10
  59.5 7.5 %collective-permute-done.1 = f32[128,768]{1,0:T(8,128)} collective-permute-done((f32[128,768]{1,0:T(8,128)}, f32[128,768]{1,0:T(8,128)}, u32[]{:S(2)}, u32[]{:S(2)}) %collective-permute-start.1) | collective-permute-done | bytes 393248 | tf_op jit(solution)/shard_map/while/body/eval_jaxpr/ppermute | solution.py:10
  67.0 1.6 %copy.13 = bf16[128,768]{1,0:T(8,128)(2,1)} copy(bf16[128,768]{1,0:T(8,128)(2,1)} %get-tuple-element.280) | data formatting | bytes 393216 | tf_op jit(solution)/shard_map/while
  68.6 0.0 collective-permute-start
  68.6 0.0 copy-start
  68.6 2.3 %fusion.24 = bf16[128,1024]{1,0:T(8,128)(2,1)S(1)} fusion(bf16[128,768]{1,0:T(8,128)(2,1)} %copy.13, bf16[1024,768]{1,0:T(8,128)(2,1)} %get-tuple-element.296, bf16[512,1024]{1,0:T(8,128)(2,1)} %get-tuple-element.298, s32[]{:T(128)S(6)} %select_n.35), kind=kOutput, calls=%fused_computation.6.clone.1 | convolution fusion | flops 202113024 | bytes 2293764 | tf_op jit(solution)/shard_map/while/body/eval_jaxpr/dot_general | solution.py:20
  70.9 0.0 copy-done
  70.9 2.1 %convolution_add_fusion.2 = f32[128,768]{1,0:T(8,128)} fusion(f32[128,768]{1,0:T(8,128)} %get-tuple-element.281, bf16[128,1024]{1,0:T(8,128)(2,1)S(1)} %fusion.24, bf16[1024,768]{1,0:T(8,128)(2,1)S(1)} %copy-done), kind=kOutput, calls=%fused_computation.7.clone.1 | convolution fusion | flops 201424896 | bytes 2621440 | tf_op jit(solution)/shard_map/while/body/eval_jaxpr/dot_general | solution.py:31
  73.1 0.0 collective-permute-start.1
  73.1 2.0 %select_add_fusion.2 = f32[1024,768]{1,0:T(8,128)S(1)} fusion(f32[1024,768]{1,0:T(8,128)S(1)} %get-tuple-element.282, bf16[128,1024]{1,0:T(8,128)(2,1)S(1)} %fusion.24, bf16[128,768]{1,0:T(8,128)(2,1)} %copy.13, pred[]{:T(512)S(6)} %compare.4), kind=kOutput, calls=%fused_computation.clone.1 | convolution fusion | flops 202899456 | bytes 6750209 | tf_op jit(solution)/shard_map/while/body/eval_jaxpr/dot_general | solution.py:26
  75.1 2.2 %collective-permute-done = bf16[128,768]{1,0:T(8,128)(2,1)} collective-permute-done((bf16[128,768]{1,0:T(8,128)(2,1)}, bf16[128,768]{1,0:T(8,128)(2,1)}, u32[]{:S(2)}, u32[]{:S(2)}) %collective-permute-start) | collective-permute-done | bytes 196640 | tf_op jit(solution)/shard_map/while/body/eval_jaxpr/ppermute | solution.py:10
  77.3 7.5 %collective-permute-done.1 = f32[128,768]{1,0:T(8,128)} collective-permute-done((f32[128,768]{1,0:T(8,128)}, f32[128,768]{1,0:T(8,128)}, u32[]{:S(2)}, u32[]{:S(2)}) %collective-permute-start.1) | collective-permute-done | bytes 393248 | tf_op jit(solution)/shard_map/while/body/eval_jaxpr/ppermute | solution.py:10
  84.8 1.9 %copy.7 = f32[128,768]{0,1:T(8,128)} copy(f32[128,768]{1,0:T(8,128)} %get-tuple-element.182) | data formatting | bytes 786432 | tf_op jit(solution)/shard_map/while | solution.py:49
  86.8 0.0 reduce-scatter.2.cloned.1.call-update
  86.8 4.3 %subtract_convert_fusion = (bf16[1024,768]{1,0:T(8,128)(2,1)}, bf16[1024,768]{1,0:T(8,128)(2,1)}) fusion(bf16[1024,768]{1,0:T(8,128)(2,1)} %get-tuple-element.306, f32[1024,768]{1,0:T(8,128)S(1)} %get-tuple-element.181, bf16[1024,768]{1,0:T(8,128)(2,1)} %param.8), kind=kLoop, calls=%fused_computation.8 | loop fusion | flops 7077888 | bytes 9437184 | tf_op jit(solution)/shard_map/convert_element_type | solution.py:57
  91.1 28.2 %reduce-scatter.2.cloned.1.call-done = f32[128,96]{0,1:T(8,128)} async-done(((f32[128,768]{0,1:T(8,128)}), f32[128,96]{0,1:T(8,128)}) %reduce-scatter.2.cloned.1.call-update) | async-done | bytes 49168 | tf_op jit(solution)/shard_map/reduce_scatter | solution.py:53
  119.2 1.4 %convert_element_type.43 = bf16[128,96]{0,1:T(8,128)(2,1)} convert(f32[128,96]{0,1:T(8,128)} %reduce-scatter.2.cloned.1.call-done) | non-fusion elementwise | flops 12288 | bytes 73728 | tf_op jit(solution)/shard_map/convert_element_type | solution.py:53
  (2 shorter events, 0.0 us)
Async XLA Ops:
  7.2 112.1 %reduce-scatter.2.cloned.1.call-start = ((), (), s32[]{:S(2)}) async-start(), calls=%async_computation.1 | async-start | bytes 442368 | tf_op jit(solution)/shard_map/reduce_scatter | solution.py:53
  11.2 11.1 %collective-permute-start = (bf16[128,768]{1,0:T(8,128)(2,1)}, bf16[128,768]{1,0:T(8,128)(2,1)}, u32[]{:S(2)}, u32[]{:S(2)}) collective-permute-start(bf16[128,768]{1,0:T(8,128)(2,1)} %copy.13), channel_id=1, source_target_pairs={{3,0},{0,1},{1,2},{2,3},{7,4},{4,5},{5,6},{6,7},{11,8},{8,9},{9,10... | collective-permute-start | bytes 589832 | tf_op jit(solution)/shard_map/while/body/eval_jaxpr/ppermute | solution.py:10
  14.2 2.3 %copy-start = (bf16[1024,768]{1,0:T(8,128)(2,1)S(1)}, bf16[1024,768]{1,0:T(8,128)(2,1)}, u32[]{:S(2)}) copy-start(bf16[1024,768]{1,0:T(8,128)(2,1)} %get-tuple-element.296) | copy-start | bytes 4718596 | tf_op jit(solution)/shard_map/while
  18.7 12.7 %collective-permute-start.1 = (f32[128,768]{1,0:T(8,128)}, f32[128,768]{1,0:T(8,128)}, u32[]{:S(2)}, u32[]{:S(2)}) collective-permute-start(f32[128,768]{1,0:T(8,128)} %convolution_add_fusion.2), channel_id=1, source_target_pairs={{3,0},{0,1},{1,2},{2,3},{7,4},{4,5},{5,6},{6,7},{11,8},{8,9},{9,10... | collective-permute-start | bytes 1179656 | tf_op jit(solution)/shard_map/while/body/eval_jaxpr/ppermute | solution.py:10
  33.0 7.8 %collective-permute-start = (bf16[128,768]{1,0:T(8,128)(2,1)}, bf16[128,768]{1,0:T(8,128)(2,1)}, u32[]{:S(2)}, u32[]{:S(2)}) collective-permute-start(bf16[128,768]{1,0:T(8,128)(2,1)} %copy.13), channel_id=1, source_target_pairs={{3,0},{0,1},{1,2},{2,3},{7,4},{4,5},{5,6},{6,7},{11,8},{8,9},{9,10... | collective-permute-start | bytes 589832 | tf_op jit(solution)/shard_map/while/body/eval_jaxpr/ppermute | solution.py:10
  33.0 2.3 %copy-start = (bf16[1024,768]{1,0:T(8,128)(2,1)S(1)}, bf16[1024,768]{1,0:T(8,128)(2,1)}, u32[]{:S(2)}) copy-start(bf16[1024,768]{1,0:T(8,128)(2,1)} %get-tuple-element.296) | copy-start | bytes 4718596 | tf_op jit(solution)/shard_map/while
  37.4 11.8 %collective-permute-start.1 = (f32[128,768]{1,0:T(8,128)}, f32[128,768]{1,0:T(8,128)}, u32[]{:S(2)}, u32[]{:S(2)}) collective-permute-start(f32[128,768]{1,0:T(8,128)} %convolution_add_fusion.2), channel_id=1, source_target_pairs={{3,0},{0,1},{1,2},{2,3},{7,4},{4,5},{5,6},{6,7},{11,8},{8,9},{9,10... | collective-permute-start | bytes 1179656 | tf_op jit(solution)/shard_map/while/body/eval_jaxpr/ppermute | solution.py:10
  50.8 8.7 %collective-permute-start = (bf16[128,768]{1,0:T(8,128)(2,1)}, bf16[128,768]{1,0:T(8,128)(2,1)}, u32[]{:S(2)}, u32[]{:S(2)}) collective-permute-start(bf16[128,768]{1,0:T(8,128)(2,1)} %copy.13), channel_id=1, source_target_pairs={{3,0},{0,1},{1,2},{2,3},{7,4},{4,5},{5,6},{6,7},{11,8},{8,9},{9,10... | collective-permute-start | bytes 589832 | tf_op jit(solution)/shard_map/while/body/eval_jaxpr/ppermute | solution.py:10
  50.8 2.3 %copy-start = (bf16[1024,768]{1,0:T(8,128)(2,1)S(1)}, bf16[1024,768]{1,0:T(8,128)(2,1)}, u32[]{:S(2)}) copy-start(bf16[1024,768]{1,0:T(8,128)(2,1)} %get-tuple-element.296) | copy-start | bytes 4718596 | tf_op jit(solution)/shard_map/while
  55.2 11.8 %collective-permute-start.1 = (f32[128,768]{1,0:T(8,128)}, f32[128,768]{1,0:T(8,128)}, u32[]{:S(2)}, u32[]{:S(2)}) collective-permute-start(f32[128,768]{1,0:T(8,128)} %convolution_add_fusion.2), channel_id=1, source_target_pairs={{3,0},{0,1},{1,2},{2,3},{7,4},{4,5},{5,6},{6,7},{11,8},{8,9},{9,10... | collective-permute-start | bytes 1179656 | tf_op jit(solution)/shard_map/while/body/eval_jaxpr/ppermute | solution.py:10
  68.6 8.7 %collective-permute-start = (bf16[128,768]{1,0:T(8,128)(2,1)}, bf16[128,768]{1,0:T(8,128)(2,1)}, u32[]{:S(2)}, u32[]{:S(2)}) collective-permute-start(bf16[128,768]{1,0:T(8,128)(2,1)} %copy.13), channel_id=1, source_target_pairs={{3,0},{0,1},{1,2},{2,3},{7,4},{4,5},{5,6},{6,7},{11,8},{8,9},{9,10... | collective-permute-start | bytes 589832 | tf_op jit(solution)/shard_map/while/body/eval_jaxpr/ppermute | solution.py:10
  68.6 2.3 %copy-start = (bf16[1024,768]{1,0:T(8,128)(2,1)S(1)}, bf16[1024,768]{1,0:T(8,128)(2,1)}, u32[]{:S(2)}) copy-start(bf16[1024,768]{1,0:T(8,128)(2,1)} %get-tuple-element.296) | copy-start | bytes 4718596 | tf_op jit(solution)/shard_map/while
  73.1 11.8 %collective-permute-start.1 = (f32[128,768]{1,0:T(8,128)}, f32[128,768]{1,0:T(8,128)}, u32[]{:S(2)}, u32[]{:S(2)}) collective-permute-start(f32[128,768]{1,0:T(8,128)} %convolution_add_fusion.2), channel_id=1, source_target_pairs={{3,0},{0,1},{1,2},{2,3},{7,4},{4,5},{5,6},{6,7},{11,8},{8,9},{9,10... | collective-permute-start | bytes 1179656 | tf_op jit(solution)/shard_map/while/body/eval_jaxpr/ppermute | solution.py:10
Sparse Core Ops, SparseCore 0:
  86.9 32.2 reduce-scatter.1
where the time goes:
time: 128 us; the launch traced here: 127 us
  waiting for transfers between devices  64.6 us (50%)
  matrix products  25.8 us (20%)
  between operations  14 us (11%)
  local copies, waits for them, and re-layouts  10.8 us (8%)
  starting transfers between devices  6.4 us (5%)
  other arithmetic  5.69 us (4%)
    ppermute x8, waiting for transfers between devices, shifted(): return lax.ppermute(block, axis, route)  36.4 us
    reduce_scatter x1, waiting for transfers between devices, shards(): lax.psum_scatter(moving, 'wide', scatter_dimension=1, tiled=True)  28.2 us
    dot_general x4, matrix products, errors_of(): lax.dot_general(row_block, weights, (((1,), (1,)), ((), ())), preferred_e...  9.14 us
    dot_general x4, matrix products, back_part(): return jnp.dot(error_rows, weights, preferred_element_type=jnp.float32)  8.49 us
    dot_general x4, matrix products, weight_part(): lax.dot_general(error_rows, row_block, (((0,), (0,)), ((), ())), preferre...  8.19 us
    while x12, local copies, waits for them, and re-layouts  6.48 us
    ppermute x8, starting transfers between devices, shifted(): return lax.ppermute(block, axis, route)  6.36 us
    convert_element_type x1, other arithmetic, shards(): (weights.astype(jnp.float32) - 0.002 * new_momentum.astype(jnp.float32))....  4.28 us
  transfers between devices with their start and end apart: 9, of which 7 were waited for; matrix products, arithmetic and copies ran while one was open for 24% of the time, Pallas kernels for 0%

commit v1 on v0

v1 whole, which is shorter than its diff:
```python
import functools

import jax
import jax.numpy as jnp
from jax import lax
from jax.experimental import pallas as pl
from jax.experimental.pallas import tpu as pltpu
from jax.sharding import PartitionSpec as P

F32 = jnp.float32
BF16 = jnp.bfloat16
MESH = pl.DeviceIdType.MESH


def mult(value, by):
    return value if isinstance(value, int) else pl.multiple_of(value, by)


def kernel(
    nw, nb, split,
    feat_ref, w_hbm, m_hbm, t_hbm,
    ow_hbm, om_hbm, fg_ref,
    feat, w_v, m_v, t_v, tt, wt, err,
    a_send, a_recv, part, b_send, b_recv, c_send, c_own, c_recv, ow_v, om_v,
    load_sem, store_sem, zs, zr, ps, pr, cs, cr, as_, ar, bs, br, xs, xr,
):
    rows = feat_ref.shape[0]
    labels, width = w_hbm.shape
    chips = nw // 2
    bw = width // nw
    pairs = nb // 2
    half = rows // 2
    piece = half // split

    wide = lax.axis_index("wide")
    blk = lax.axis_index("blk")
    core = lax.rem(wide, 2)
    chip = lax.div(wide, 2)
    mate_core = 1 - core
    partner = chip * 2 + mate_core
    slot = lax.rem(chip, split)
    group = chip - slot
    pair = lax.div(blk, 2)
    mate = pair * 2 + 1 - lax.rem(blk, 2)

    def pair_at(i):
        return lax.rem(pair + i, pairs)

    sources = [mate]
    for i in range(1, pairs):
        sources += [pair_at(i) * 2, pair_at(i) * 2 + 1]
    targets_z = [mate]
    for i in range(1, pairs):
        back = lax.rem(pair - i + pairs, pairs)
        targets_z += [back * 2, back * 2 + 1]

    def feat_at(block, first, count):
        start = lax.rem(block, 2) * rows + first
        return feat.at[lax.div(block, 2), pl.ds(mult(start, 16), count)]

    loads = [
        pltpu.make_async_copy(feat_ref, feat_at(blk, 0, rows), load_sem.at[0]),
        pltpu.make_async_copy(w_hbm, w_v, load_sem.at[1]),
        pltpu.make_async_copy(t_hbm, t_v, load_sem.at[2]),
        pltpu.make_async_copy(m_hbm, m_v, load_sem.at[3]),
    ]
    for load in loads:
        load.start()

    barrier = pltpu.get_barrier_semaphore()
    peers = [(partner, blk)]
    peers += [(lax.rem(chip + d, chips) * 2 + core, blk) for d in range(1, chips)]
    peers += [(wide, lax.rem(blk + d, nb)) for d in range(1, nb)]
    for peer in peers:
        pl.semaphore_signal(barrier, inc=1, device_id=peer, device_id_type=MESH)
    pl.semaphore_wait(barrier, len(peers))

    def remote(src, dst, send, recv, peer):
        return pltpu.make_async_remote_copy(
            src_ref=src, dst_ref=dst, send_sem=send, recv_sem=recv,
            device_id=peer, device_id_type=MESH,
        )

    sent = []
    mine = core * half + slot * piece

    for target in targets_z:
        copy = remote(
            feat_ref.at[pl.ds(mult(mine, 16), piece)], feat_at(blk, mine, piece),
            zs.at[target], zr.at[blk], (wide, target),
        )
        copy.start()
        sent.append(copy)

    def spread(source):
        here = feat_at(source, mine, piece)
        remote(here, here, zs.at[source], zr.at[source], (wide, source)).wait_recv()
        for d in range(1, split):
            other = lax.rem(slot + d, split)
            copy = remote(
                here, here, ps.at[source, other], pr.at[source, slot],
                ((group + other) * 2 + core, blk),
            )
            copy.start()
            sent.append(copy)

    def cross(source):
        for d in range(1, split):
            other = lax.rem(slot + d, split)
            there = feat_at(source, core * half + other * piece, piece)
            remote(
                there, there, ps.at[source, other], pr.at[source, other],
                ((group + other) * 2 + core, blk),
            ).wait_recv()
        lot = feat_at(source, core * half, half)
        copy = remote(lot, lot, cs.at[source], cr.at[source], (partner, blk))
        copy.start()
        sent.append(copy)

    def arrived(source):
        lot = feat_at(source, mate_core * half, half)
        remote(lot, lot, cs.at[source], cr.at[source], (partner, blk)).wait_recv()

    def turn_weights(first, last):
        for c in range(first, last):
            turned = w_v[:, 128 * c:128 * (c + 1)].T
            at = 128 * c
            while at < 128 * (c + 1):
                block, off = at // bw, at % bw
                count = min(bw - off, 128 * (c + 1) - at)
                to = (block // 2) * bw + off
                wt[block % 2, to:to + count, :] = turned[at - 128 * c:at - 128 * c + count]
                at += count

    def turn_targets(i):
        p = pair_at(i)
        first = mult(p * 2 * rows, 2 * rows)
        tt[p] = t_v[pl.ds(first, 2 * rows), :].T

    tiles = width // 128
    loads[1].wait()
    turn_weights(0, tiles // 2)
    spread(sources[0])
    turn_weights(tiles // 2, tiles)
    for source in sources[1:]:
        spread(source)
    cross(sources[0])
    loads[2].wait()
    turn_targets(0)
    for source in sources[1:]:
        cross(source)
    for i in range(1, pairs):
        turn_targets(i)
    loads[0].wait()

    step = min(512, labels)

    def errors(i):
        p = pair_at(i)
        for first in range(0, labels, step):
            scores = lax.dot_general(
                w_v[first:first + step], feat[p], (((1,), (1,)), ((), ())),
                preferred_element_type=F32,
            )
            chance = 0.5 * jnp.tanh(0.5 * scores) + 0.5
            err[p, first:first + step] = (
                chance - tt[p, first:first + step].astype(F32)
            ).astype(BF16)

    def back(p, which):
        return jnp.dot(wt[which], err[p], preferred_element_type=F32)

    def pair_copy(p):
        return remote(a_send.at[p], a_recv.at[p], as_.at[p], ar.at[p], (partner, blk))

    def first_half(i):
        p = pair_at(i)
        a_send[p] = back(p, mate_core).astype(BF16)
        copy = pair_copy(p)
        copy.start()
        sent.append(copy)

    def second_half(i):
        p = pair_at(i)
        part[p] = back(p, core).reshape(chips, bw, 2 * rows)

    def to_chips(i):
        p = pair_at(i)
        pair_copy(p).wait_recv()
        total = part[p] + a_recv[p].astype(F32).reshape(chips, bw, 2 * rows)
        part[p] = total
        b_send[p] = total.astype(BF16)
        for d in range(1, chips):
            other = lax.rem(chip + d, chips)
            copy = remote(
                b_send.at[p, other], b_recv.at[p, chip], bs.at[p, other], br.at[p, chip],
                (other * 2 + core, blk),
            )
            copy.start()
            sent.append(copy)

    def to_blocks(i):
        p = pair_at(i)
        total = part[p, chip]
        for d in range(1, chips):
            other = lax.rem(chip + d, chips)
            remote(
                b_send.at[p, other], b_recv.at[p, other], bs.at[p, other], br.at[p, other],
                (other * 2 + core, blk),
            ).wait_recv()
            total = total + b_recv[p, other].astype(F32)
        for n in range(2):
            c_own[p * 2 + n] = total[:, n * rows:(n + 1) * rows]
            c_send[p * 2 + n] = total[:, n * rows:(n + 1) * rows].astype(BF16)
        for target in [mate] if i == 0 else [p * 2, p * 2 + 1]:
            copy = remote(
                c_send.at[target], c_recv.at[blk], xs.at[target], xr.at[blk], (wide, target)
            )
            copy.start()
            sent.append(copy)

    stores = []
    chunk = min(256, labels)

    def update(n):
        first = n * chunk
        span = slice(first, first + chunk)
        grad = jnp.dot(err[0, span], feat[0], preferred_element_type=F32)
        for p in range(1, pairs):
            grad = grad + jnp.dot(err[p, span], feat[p], preferred_element_type=F32)
        moment = (0.9 * m_v[span].astype(F32) + grad).astype(BF16)
        om_v[span] = moment
        ow_v[span] = (w_v[span].astype(F32) - 0.002 * moment.astype(F32)).astype(BF16)
        for k, (src, dst) in enumerate(((om_v, om_hbm), (ow_v, ow_hbm))):
            copy = pltpu.make_async_copy(
                src.at[pl.ds(first, chunk)], dst.at[pl.ds(first, chunk)], store_sem.at[k, n]
            )
            copy.start()
            stores.append(copy)

    updates = list(range(labels // chunk))

    def some_updates(count):
        for n in updates[:count]:
            update(n)
        del updates[:count]

    arrived(sources[0])
    errors(0)
    first_half(0)
    second_half(0)
    for i in range(1, pairs):
        arrived(sources[2 * i - 1])
        arrived(sources[2 * i])
        errors(i)
        first_half(i)
        to_chips(i - 1)
        second_half(i)
        if i >= 2:
            to_blocks(i - 2)
    to_chips(pairs - 1)
    loads[3].wait()
    some_updates(1)
    if pairs >= 2:
        to_blocks(pairs - 2)
    some_updates(2)
    to_blocks(pairs - 1)
    some_updates(len(updates))

    total = c_own[blk]
    for d in range(1, nb):
        other = lax.rem(blk + d, nb)
        remote(
            c_send.at[other], c_recv.at[other], xs.at[other], xr.at[other], (wide, other)
        ).wait_recv()
        total = total + c_recv[other].astype(F32)
    fg_ref[...] = total.T.astype(BF16)

    for copy in sent:
        copy.wait_send()
    for copy in stores:
        copy.wait()


def solution(mesh):
    nw, nb = mesh.shape["wide"], mesh.shape["blk"]
    chips = nw // 2

    def shards(features, weights, momentum, targets):
        rows, width = features.shape
        labels = weights.shape[0]
        split = chips
        while split > 1 and (chips % split or rows % (32 * split)):
            split -= 1
        bw = width // nw
        pairs = nb // 2
        total_rows = targets.shape[0]
        flops = 6 * total_rows * labels * width
        hbm = pl.BlockSpec(memory_space=pl.ANY)
        vmem = pl.BlockSpec(memory_space=pltpu.VMEM)
        dma = pltpu.SemaphoreType.DMA
        chunks = labels // min(256, labels)
        new_weights, new_momentum, feature_grad = pl.pallas_call(
            functools.partial(kernel, nw, nb, split),
            out_shape=(
                jax.ShapeDtypeStruct(weights.shape, BF16),
                jax.ShapeDtypeStruct(momentum.shape, BF16),
                jax.ShapeDtypeStruct((rows, bw), BF16),
            ),
            in_specs=[hbm, hbm, hbm, hbm],
            out_specs=(hbm, hbm, vmem),
            scratch_shapes=[
                pltpu.VMEM((pairs, 2 * rows, width), BF16),
                pltpu.VMEM((labels, width), BF16),
                pltpu.VMEM((labels, width), BF16),
                pltpu.VMEM((total_rows, labels), BF16),
                pltpu.VMEM((pairs, labels, 2 * rows), BF16),
                pltpu.VMEM((2, width // 2, labels), BF16),
                pltpu.VMEM((pairs, labels, 2 * rows), BF16),
                pltpu.VMEM((pairs, width // 2, 2 * rows), BF16),
                pltpu.VMEM((pairs, width // 2, 2 * rows), BF16),
                pltpu.VMEM((pairs, chips, bw, 2 * rows), F32),
                pltpu.VMEM((pairs, chips, bw, 2 * rows), BF16),
                pltpu.VMEM((pairs, chips, bw, 2 * rows), BF16),
                pltpu.VMEM((nb, bw, rows), BF16),
                pltpu.VMEM((nb, bw, rows), F32),
                pltpu.VMEM((nb, bw, rows), BF16),
                pltpu.VMEM((labels, width), BF16),
                pltpu.VMEM((labels, width), BF16),
                dma((4,)), dma((2, chunks)),
                dma((nb,)), dma((nb,)),
                dma((nb, split)), dma((nb, split)),
                dma((nb,)), dma((nb,)),
                dma((pairs,)), dma((pairs,)),
                dma((pairs, chips)), dma((pairs, chips)),
                dma((nb,)), dma((nb,)),
            ],
            compiler_params=pltpu.CompilerParams(
                collective_id=0, has_side_effects=True, vmem_limit_bytes=56 * 1024 * 1024
            ),
            cost_estimate=pl.CostEstimate(
                flops=flops, bytes_accessed=8 * labels * width, transcendentals=total_rows * labels
            ),
        )(features, weights, momentum, targets)
        return new_weights, new_momentum, feature_grad

    placed = (
        P("blk", None),
        P(("wide", "blk"), None),
        P(("wide", "blk"), None),
        P(None, ("wide", "blk")),
    )
    return jax.shard_map(
        shards,
        mesh=mesh,
        in_specs=placed,
        out_specs=(P(("wide", "blk"), None), P(("wide", "blk"), None), P("blk", "wide")),
        check_vma=False,
    )
```

time: 128 us -> 34.6 us (0.27)
  waiting for transfers between devices: 64.6 us -> 0 us
  Pallas kernels: 0 us -> 28.4 us
  matrix products: 25.8 us -> 0 us
  between operations: 14 us -> 0.64 us
  starting transfers between devices: 6.4 us -> 0 us
  other arithmetic: 5.69 us -> 0 us
  local copies, waits for them, and re-layouts: 10.8 us -> 5.38 us
    ppermute x8 -> x0, waiting for transfers between devices: 36.4 us -> none  [shifted(): return lax.ppermute(block, axis, route)]
    pallas_call x0 -> x1, Pallas kernels: none -> 28.4 us  [shards(): pl.pallas_call(functools.partial(kernel, nw, nb, split), out_shape=(jax.S...]
    reduce_scatter x1 -> x0, waiting for transfers between devices: 28.2 us -> none  [shards(): lax.psum_scatter(moving, 'wide', scatter_dimension=1, tiled=True)]
    dot_general x12 -> x0, matrix products: 25.8 us -> none  [the longest x4 9.14 us: errors_of(): lax.dot_general(row_block, weights, (((1,), (1,)), ((), ())), preferred_e...]
    while x13 -> x0, local copies, waits for them, and re-layouts: 8.39 us -> none
    ppermute x8 -> x0, starting transfers between devices: 6.36 us -> none  [shifted(): return lax.ppermute(block, axis, route)]
    convert_element_type x2 -> x0, other arithmetic: 5.69 us -> none  [the longest x1 4.28 us: shards(): (weights.astype(jnp.float32) - 0.002 * new_momentum.astype(jnp.float32))....]
    unnamed x1 -> x4, local copies, waits for them, and re-layouts: 1.62 us -> 3.92 us
  transfers between devices with their start and end apart: 9 -> 0, of which waited for: 7 -> 0; matrix products, arithmetic and copies ran while one was open for 24% -> 0% of each run, Pallas kernels for 0% -> 0%
where the time goes in v1:
time: 34.6 us; the launch traced here: 34.5 us
  Pallas kernels  28.4 us (82%)
  local copies, waits for them, and re-layouts  5.38 us (16%)
  between operations  0.64 us (2%)
    pallas_call x1, Pallas kernels, shards(): pl.pallas_call(functools.partial(kernel, nw, nb, split), out_shape=(jax.S...  28.4 us
    unnamed x4, local copies, waits for them, and re-layouts  3.92 us
    pallas_call x1, local copies, waits for them, and re-layouts, shards(): pl.pallas_call(functools.partial(kernel, nw, nb, split), out_shape=(jax.S...  1.46 us

profile of v1, /device:TPU:0, one launch (start us, length us, event | category | flops | bytes accessed | tf_op | source)
XLA Modules:
  0.0 34.5 jit_solution(10550436639226993477)
XLA Ops:
  0.6 28.4 %shard_map.67 = (bf16[1024,768]{1,0:T(8,128)(2,1)}, bf16[1024,768]{1,0:T(8,128)(2,1)}, bf16[128,96]{1,0:T(8,128)(2,1)}) custom-call(bf16[128,768]{1,0:T(8,128)(2,1)} %feat_ref.1, bf16[1024,768]{1,0:T(8,128)(2,1)} %w_hbm.1, bf16[1024,768]{1,0:T(8,128)(2,1)} %m_hbm.1, bf16[512,1024]{1,0:T(8,128)(2,1)} %t_hbm.1), custom_call_target="tpu_custom_call" | custom-call | flops 2415919104 | bytes 6291456 | tf_op jit(solution)/shard_map/pallas_call | solution.py:303
  29.1 1.5 %copy.7 = bf16[128,96]{0,1:T(8,128)(2,1)} copy(bf16[128,96]{1,0:T(8,128)(2,1)} %get-tuple-element.5) | data formatting | bytes 49152 | tf_op jit(solution)/shard_map/pallas_call | solution.py:303
  30.5 0.0 copy-start
  30.5 2.8 %copy.10 = bf16[1024,768]{1,0:T(8,128)(2,1)} copy(bf16[1024,768]{1,0:T(8,128)(2,1)} %get-tuple-element.9) | data formatting | bytes 3145728
  33.3 0.0 copy-done
  33.3 1.1 %copy.11 = bf16[1024,768]{1,0:T(8,128)(2,1)} copy(bf16[1024,768]{1,0:T(8,128)(2,1)S(1)} %copy-done) | data formatting | bytes 3145728
Async XLA Ops:
  30.5 2.8 %copy-start = (bf16[1024,768]{1,0:T(8,128)(2,1)S(1)}, bf16[1024,768]{1,0:T(8,128)(2,1)}, u32[]{:S(2)}) copy-start(bf16[1024,768]{1,0:T(8,128)(2,1)} %get-tuple-element.10) | copy-start | bytes 4718596

commit v2 on v1

--- a/solution.py
+++ b/solution.py
@@ -19,10 +19,10 @@
 def kernel(
     nw, nb, split,
     feat_ref, w_hbm, m_hbm, t_hbm,
-    ow_hbm, om_hbm, fg_ref,
+    ow_v, om_v, fg_ref,
     feat, w_v, m_v, t_v, tt, wt, err,
-    a_send, a_recv, part, b_send, b_recv, c_send, c_own, c_recv, ow_v, om_v,
-    load_sem, store_sem, zs, zr, ps, pr, cs, cr, as_, ar, bs, br, xs, xr,
+    a_send, a_recv, part, b_send, b_recv, c_send, c_own, c_recv,
+    load_sem, zs, zr, ps, pr, cs, cr, as_, ar, bs, br, xs, xr,
 ):
     rows = feat_ref.shape[0]
     labels, width = w_hbm.shape
@@ -139,17 +139,17 @@
 
     tiles = width // 128
     loads[1].wait()
-    turn_weights(0, tiles // 2)
+    turn_weights(0, tiles // 3)
     spread(sources[0])
-    turn_weights(tiles // 2, tiles)
+    turn_weights(tiles // 3, tiles // 2)
     for source in sources[1:]:
         spread(source)
     cross(sources[0])
-    loads[2].wait()
-    turn_targets(0)
+    turn_weights(tiles // 2, tiles)
     for source in sources[1:]:
         cross(source)
-    for i in range(1, pairs):
+    loads[2].wait()
+    for i in range(pairs):
         turn_targets(i)
     loads[0].wait()
 
@@ -219,7 +219,6 @@
             copy.start()
             sent.append(copy)
 
-    stores = []
     chunk = min(256, labels)
 
     def update(n):
@@ -231,12 +230,6 @@
         moment = (0.9 * m_v[span].astype(F32) + grad).astype(BF16)
         om_v[span] = moment
         ow_v[span] = (w_v[span].astype(F32) - 0.002 * moment.astype(F32)).astype(BF16)
-        for k, (src, dst) in enumerate(((om_v, om_hbm), (ow_v, ow_hbm))):
-            copy = pltpu.make_async_copy(
-                src.at[pl.ds(first, chunk)], dst.at[pl.ds(first, chunk)], store_sem.at[k, n]
-            )
-            copy.start()
-            stores.append(copy)
 
     updates = list(range(labels // chunk))
 
@@ -274,12 +267,10 @@
             c_send.at[other], c_recv.at[other], xs.at[other], xr.at[other], (wide, other)
         ).wait_recv()
         total = total + c_recv[other].astype(F32)
-    fg_ref[...] = total.T.astype(BF16)
+    fg_ref[...] = total.astype(BF16)
 
     for copy in sent:
         copy.wait_send()
-    for copy in stores:
-        copy.wait()
 
 
 def solution(mesh):
@@ -299,16 +290,15 @@
         hbm = pl.BlockSpec(memory_space=pl.ANY)
         vmem = pl.BlockSpec(memory_space=pltpu.VMEM)
         dma = pltpu.SemaphoreType.DMA
-        chunks = labels // min(256, labels)
         new_weights, new_momentum, feature_grad = pl.pallas_call(
             functools.partial(kernel, nw, nb, split),
             out_shape=(
-                jax.ShapeDtypeStruct(weights.shape, BF16),
-                jax.ShapeDtypeStruct(momentum.shape, BF16),
-                jax.ShapeDtypeStruct((rows, bw), BF16),
+                pltpu.VMEM(weights.shape, BF16),
+                pltpu.VMEM(momentum.shape, BF16),
+                pltpu.VMEM((bw, rows), BF16),
             ),
             in_specs=[hbm, hbm, hbm, hbm],
-            out_specs=(hbm, hbm, vmem),
+            out_specs=(vmem, vmem, vmem),
             scratch_shapes=[
                 pltpu.VMEM((pairs, 2 * rows, width), BF16),
                 pltpu.VMEM((labels, width), BF16),
@@ -325,9 +315,7 @@
                 pltpu.VMEM((nb, bw, rows), BF16),
                 pltpu.VMEM((nb, bw, rows), F32),
                 pltpu.VMEM((nb, bw, rows), BF16),
-                pltpu.VMEM((labels, width), BF16),
-                pltpu.VMEM((labels, width), BF16),
-                dma((4,)), dma((2, chunks)),
+                dma((4,)),
                 dma((nb,)), dma((nb,)),
                 dma((nb, split)), dma((nb, split)),
                 dma((nb,)), dma((nb,)),
@@ -342,7 +330,7 @@
                 flops=flops, bytes_accessed=8 * labels * width, transcendentals=total_rows * labels
             ),
         )(features, weights, momentum, targets)
-        return new_weights, new_momentum, feature_grad
+        return new_weights, new_momentum, feature_grad.T
 
     placed = (
         P("blk", None),

time: 34.6 us -> 31.4 us (0.908)
  local copies, waits for them, and re-layouts: 5.38 us -> 2.89 us
  Pallas kernels: 28.4 us -> 27.8 us
    pallas_call x1 -> x0, local copies, waits for them, and re-layouts: 1.46 us -> none  [shards(): pl.pallas_call(functools.partial(kernel, nw, nb, split), out_shape=(jax.S...]
    unnamed x4 -> x3, local copies, waits for them, and re-layouts: 3.92 us -> 2.89 us
    pallas_call x1, Pallas kernels: 28.4 us -> 27.8 us  [shards(): pl.pallas_call(functools.partial(kernel, nw, nb, split), out_shape=(pltpu...]
where the time goes in v2:
time: 31.4 us; the launch traced here: 31.3 us
  Pallas kernels  27.8 us (89%)
  local copies, waits for them, and re-layouts  2.89 us (9%)
  between operations  0.64 us (2%)
    pallas_call x1, Pallas kernels, shards(): pl.pallas_call(functools.partial(kernel, nw, nb, split), out_shape=(pltpu...  27.8 us
    unnamed x3, local copies, waits for them, and re-layouts  2.89 us

profile of v2, /device:TPU:0, one launch (start us, length us, event | category | flops | bytes accessed | tf_op | source)
XLA Modules:
  0.0 31.3 jit_solution(4323974924864339166)
XLA Ops:
  0.6 27.8 %shard_map.67 = (bf16[1024,768]{1,0:T(8,128)(2,1)S(1)}, bf16[1024,768]{1,0:T(8,128)(2,1)S(1)}, bf16[96,128]{1,0:T(8,128)(2,1)S(1)}) custom-call(bf16[128,768]{1,0:T(8,128)(2,1)} %feat_ref.1, bf16[1024,768]{1,0:T(8,128)(2,1)} %w_hbm.1, bf16[1024,768]{1,0:T(8,128)(2,1)} %m_hbm.1, bf16[512,1024]{1,0:T(8,128)(2,1)} %t_hbm.1), custom_call_target="tpu_custom_call" | custom-call | flops 2415919104 | bytes 6291456 | tf_op jit(solution)/shard_map/pallas_call | solution.py:293
  28.4 1.1 %copy.10 = bf16[1024,768]{1,0:T(8,128)(2,1)} copy(bf16[1024,768]{1,0:T(8,128)(2,1)S(1)} %get-tuple-element.9) | data formatting | bytes 3145728
  29.5 0.6 %copy.12 = bf16[128,96]{0,1:T(8,128)(2,1)} copy(bf16[128,96]{0,1:T(8,128)(2,1)S(1)} %bitcast.1) | data formatting | bytes 49152
  30.2 1.1 %copy.11 = bf16[1024,768]{1,0:T(8,128)(2,1)} copy(bf16[1024,768]{1,0:T(8,128)(2,1)S(1)} %get-tuple-element.10) | data formatting | bytes 3145728

commit v3 on v2

--- a/solution.py
+++ b/solution.py
@@ -10,6 +10,7 @@
 F32 = jnp.float32
 BF16 = jnp.bfloat16
 MESH = pl.DeviceIdType.MESH
+parts = 4
 
 
 def mult(value, by):
@@ -21,7 +22,7 @@
     feat_ref, w_hbm, m_hbm, t_hbm,
     ow_v, om_v, fg_ref,
     feat, w_v, m_v, t_v, tt, wt, err,
-    a_send, a_recv, part, b_send, b_recv, c_send, c_own, c_recv,
+    a_send, a_recv, part, b_send, b_recv, c_send, c_recv,
     load_sem, zs, zr, ps, pr, cs, cr, as_, ar, bs, br, xs, xr,
 ):
     rows = feat_ref.shape[0]
@@ -182,40 +183,46 @@
 
     def second_half(i):
         p = pair_at(i)
-        part[p] = back(p, core).reshape(chips, bw, 2 * rows)
+        mine_part = back(p, core)
+        for n in range(2):
+            part[p * 2 + n] = mine_part[:, n * rows:(n + 1) * rows].reshape(chips, bw, rows)
+
+    def blocks_of(i):
+        return [mate, blk] if i == 0 else [pair_at(i) * 2, pair_at(i) * 2 + 1]
 
     def to_chips(i):
         p = pair_at(i)
         pair_copy(p).wait_recv()
-        total = part[p] + a_recv[p].astype(F32).reshape(chips, bw, 2 * rows)
-        part[p] = total
-        b_send[p] = total.astype(BF16)
-        for d in range(1, chips):
-            other = lax.rem(chip + d, chips)
-            copy = remote(
-                b_send.at[p, other], b_recv.at[p, chip], bs.at[p, other], br.at[p, chip],
-                (other * 2 + core, blk),
-            )
-            copy.start()
-            sent.append(copy)
-
-    def to_blocks(i):
-        p = pair_at(i)
-        total = part[p, chip]
+        for n in range(2):
+            theirs = a_recv[p, :, n * rows:(n + 1) * rows].astype(F32)
+            total = part[p * 2 + n] + theirs.reshape(chips, bw, rows)
+            part[p * 2 + n] = total
+            b_send[p * 2 + n] = total.astype(BF16)
+        for q in blocks_of(i):
+            for d in range(1, chips):
+                other = lax.rem(chip + d, chips)
+                copy = remote(
+                    b_send.at[q, other], b_recv.at[q, chip], bs.at[q, other], br.at[q, chip],
+                    (other * 2 + core, blk),
+                )
+                copy.start()
+                sent.append(copy)
+
+    def block_sum(q):
+        total = part[q, chip]
         for d in range(1, chips):
             other = lax.rem(chip + d, chips)
             remote(
-                b_send.at[p, other], b_recv.at[p, other], bs.at[p, other], br.at[p, other],
+                b_send.at[q, other], b_recv.at[q, other], bs.at[q, other], br.at[q, other],
                 (other * 2 + core, blk),
             ).wait_recv()
-            total = total + b_recv[p, other].astype(F32)
-        for n in range(2):
-            c_own[p * 2 + n] = total[:, n * rows:(n + 1) * rows]
-            c_send[p * 2 + n] = total[:, n * rows:(n + 1) * rows].astype(BF16)
-        for target in [mate] if i == 0 else [p * 2, p * 2 + 1]:
-            copy = remote(
-                c_send.at[target], c_recv.at[blk], xs.at[target], xr.at[blk], (wide, target)
-            )
+            total = total + b_recv[q, other].astype(F32)
+        return total
+
+    def to_blocks(i):
+        for q in [mate] if i == 0 else blocks_of(i):
+            c_send[q] = block_sum(q).astype(BF16)
+            copy = remote(c_send.at[q], c_recv.at[blk], xs.at[q], xr.at[blk], (wide, q))
             copy.start()
             sent.append(copy)
 
@@ -245,9 +252,9 @@
     for i in range(1, pairs):
         arrived(sources[2 * i - 1])
         arrived(sources[2 * i])
+        to_chips(i - 1)
         errors(i)
         first_half(i)
-        to_chips(i - 1)
         second_half(i)
         if i >= 2:
             to_blocks(i - 2)
@@ -260,7 +267,7 @@
     to_blocks(pairs - 1)
     some_updates(len(updates))
 
-    total = c_own[blk]
+    total = block_sum(blk)
     for d in range(1, nb):
         other = lax.rem(blk + d, nb)
         remote(
@@ -271,6 +278,19 @@
 
     for copy in sent:
         copy.wait_send()
+
+
+def keep(w_ref, m_ref, g_ref, w_out, m_out, g_out, sems):
+    count = w_ref.shape[0] // parts
+    copies = [pltpu.make_async_copy(g_ref, g_out, sems.at[2 * parts])]
+    for n in range(parts):
+        span = pl.ds(n * count, count)
+        copies.append(pltpu.make_async_copy(w_ref.at[span], w_out.at[span], sems.at[2 * n]))
+        copies.append(pltpu.make_async_copy(m_ref.at[span], m_out.at[span], sems.at[2 * n + 1]))
+    for copy in copies:
+        copy.start()
+    for copy in copies:
+        copy.wait()
 
 
 def solution(mesh):
@@ -309,18 +329,17 @@
                 pltpu.VMEM((pairs, labels, 2 * rows), BF16),
                 pltpu.VMEM((pairs, width // 2, 2 * rows), BF16),
                 pltpu.VMEM((pairs, width // 2, 2 * rows), BF16),
-                pltpu.VMEM((pairs, chips, bw, 2 * rows), F32),
-                pltpu.VMEM((pairs, chips, bw, 2 * rows), BF16),
-                pltpu.VMEM((pairs, chips, bw, 2 * rows), BF16),
+                pltpu.VMEM((nb, chips, bw, rows), F32),
+                pltpu.VMEM((nb, chips, bw, rows), BF16),
+                pltpu.VMEM((nb, chips, bw, rows), BF16),
                 pltpu.VMEM((nb, bw, rows), BF16),
-                pltpu.VMEM((nb, bw, rows), F32),
                 pltpu.VMEM((nb, bw, rows), BF16),
                 dma((4,)),
                 dma((nb,)), dma((nb,)),
                 dma((nb, split)), dma((nb, split)),
                 dma((nb,)), dma((nb,)),
                 dma((pairs,)), dma((pairs,)),
-                dma((pairs, chips)), dma((pairs, chips)),
+                dma((nb, chips)), dma((nb, chips)),
                 dma((nb,)), dma((nb,)),
             ],
             compiler_params=pltpu.CompilerParams(
@@ -330,6 +349,16 @@
                 flops=flops, bytes_accessed=8 * labels * width, transcendentals=total_rows * labels
             ),
         )(features, weights, momentum, targets)
+        new_weights, new_momentum, feature_grad = pl.pallas_call(
+            keep,
+            out_shape=tuple(
+                jax.ShapeDtypeStruct(shape, BF16) for shape in (weights.shape, momentum.shape, (bw, rows))
+            ),
+            in_specs=[vmem] * 3,
+            out_specs=(hbm,) * 3,
+            scratch_shapes=[dma((2 * parts + 1,))],
+            compiler_params=pltpu.CompilerParams(vmem_limit_bytes=48 * 1024 * 1024),
+        )(new_weights, new_momentum, feature_grad)
         return new_weights, new_momentum, feature_grad.T
 
     placed = (

time: 31.4 us -> 29.7 us (0.946)
  local copies, waits for them, and re-layouts: 2.89 us -> 0 us
  Pallas kernels: 27.8 us -> 28.9 us
    unnamed x3 -> x0, local copies, waits for them, and re-layouts: 2.89 us -> none
    pallas_call x0 -> x1, Pallas kernels: none -> 1.74 us  [shards(): pl.pallas_call(keep, out_shape=tuple((jax.ShapeDtypeStruct(shape, BF16) f...]
    pallas_call x1, Pallas kernels: 27.8 us -> 27.2 us  [shards(): pl.pallas_call(functools.partial(kernel, nw, nb, split), out_shape=(pltpu...]
where the time goes in v3:
time: 29.7 us; the launch traced here: 29.5 us
  Pallas kernels  28.9 us (97%)
  between operations  0.64 us (2%)
    pallas_call x1, Pallas kernels, shards(): pl.pallas_call(functools.partial(kernel, nw, nb, split), out_shape=(pltpu...  27.2 us
    pallas_call x1, Pallas kernels, shards(): pl.pallas_call(keep, out_shape=tuple((jax.ShapeDtypeStruct(shape, BF16) f...  1.74 us

profile of v3, /device:TPU:0, one launch (start us, length us, event | category | flops | bytes accessed | tf_op | source)
XLA Modules:
  0.0 29.5 jit_solution(7060107844071471555)
XLA Ops:
  0.6 27.2 %shard_map.67 = (bf16[1024,768]{1,0:T(8,128)(2,1)S(1)}, bf16[1024,768]{1,0:T(8,128)(2,1)S(1)}, bf16[96,128]{1,0:T(8,128)(2,1)S(1)}) custom-call(bf16[128,768]{1,0:T(8,128)(2,1)} %feat_ref.1, bf16[1024,768]{1,0:T(8,128)(2,1)} %w_hbm.1, bf16[1024,768]{1,0:T(8,128)(2,1)} %m_hbm.1, bf16[512,1024]{1,0:T(8,128)(2,1)} %t_hbm.1), custom_call_target="tpu_custom_call" | custom-call | flops 2415919104 | bytes 6291456 | tf_op jit(solution)/shard_map/pallas_call | solution.py:313
  27.8 1.7 %shard_map.68 = (bf16[1024,768]{1,0:T(8,128)(2,1)}, bf16[1024,768]{1,0:T(8,128)(2,1)}, bf16[96,128]{1,0:T(8,128)(2,1)}) custom-call(bf16[1024,768]{1,0:T(8,128)(2,1)S(1)} %get-tuple-element.9.w_ref, bf16[1024,768]{1,0:T(8,128)(2,1)S(1)} %get-tuple-element.10.m_ref, bf16[96,128]{1,0:T(8,128)(2,1)S(1)} %get-tuple-element.11.g_ref), custom_call_target="tpu_custom_call" | custom-call | tf_op jit(solution)/shard_map/pallas_call | solution.py:352

commit v4 on v3

--- a/solution.py
+++ b/solution.py
@@ -85,9 +85,10 @@
     sent = []
     mine = core * half + slot * piece
 
-    for target in targets_z:
+    for target in targets_z[1:] + [mate]:
+        first, count = (core * half, half) if target is mate else (mine, piece)
         copy = remote(
-            feat_ref.at[pl.ds(mult(mine, 16), piece)], feat_at(blk, mine, piece),
+            feat_ref.at[pl.ds(mult(first, 16), count)], feat_at(blk, first, count),
             zs.at[target], zr.at[blk], (wide, target),
         )
         copy.start()
@@ -106,7 +107,10 @@
             sent.append(copy)
 
     def cross(source):
-        for d in range(1, split):
+        if source is mate:
+            whole = feat_at(source, core * half, half)
+            remote(whole, whole, zs.at[source], zr.at[source], (wide, source)).wait_recv()
+        for d in range(1, 1 if source is mate else split):
             other = lax.rem(slot + d, split)
             there = feat_at(source, core * half + other * piece, piece)
             remote(
@@ -141,17 +145,13 @@
     tiles = width // 128
     loads[1].wait()
     turn_weights(0, tiles // 3)
-    spread(sources[0])
-    turn_weights(tiles // 3, tiles // 2)
     for source in sources[1:]:
         spread(source)
-    cross(sources[0])
+    turn_weights(tiles // 3, tiles // 2)
+    cross(mate)
+    loads[2].wait()
+    turn_targets(0)
     turn_weights(tiles // 2, tiles)
-    for source in sources[1:]:
-        cross(source)
-    loads[2].wait()
-    for i in range(pairs):
-        turn_targets(i)
     loads[0].wait()
 
     step = min(512, labels)
@@ -247,8 +247,12 @@
 
     arrived(sources[0])
     errors(0)
+    for source in sources[1:]:
+        cross(source)
     first_half(0)
     second_half(0)
+    for i in range(1, pairs):
+        turn_targets(i)
     for i in range(1, pairs):
         arrived(sources[2 * i - 1])
         arrived(sources[2 * i])

time: 29.7 us -> 28.9 us (0.973)
  Pallas kernels: 28.9 us -> 28.1 us
    pallas_call x1, Pallas kernels: 27.2 us -> 26.4 us  [shards(): pl.pallas_call(functools.partial(kernel, nw, nb, split), out_shape=(pltpu...]
where the time goes in v4:
time: 28.9 us; the launch traced here: 28.8 us
  Pallas kernels  28.1 us (97%)
  between operations  0.64 us (2%)
    pallas_call x1, Pallas kernels, shards(): pl.pallas_call(functools.partial(kernel, nw, nb, split), out_shape=(pltpu...  26.4 us
    pallas_call x1, Pallas kernels, shards(): pl.pallas_call(keep, out_shape=tuple((jax.ShapeDtypeStruct(shape, BF16) f...  1.74 us

profile of v4, /device:TPU:0, one launch (start us, length us, event | category | flops | bytes accessed | tf_op | source)
XLA Modules:
  0.0 28.8 jit_solution(15188566811749569765)
XLA Ops:
  0.6 26.4 %shard_map.67 = (bf16[1024,768]{1,0:T(8,128)(2,1)S(1)}, bf16[1024,768]{1,0:T(8,128)(2,1)S(1)}, bf16[96,128]{1,0:T(8,128)(2,1)S(1)}) custom-call(bf16[128,768]{1,0:T(8,128)(2,1)} %feat_ref.1, bf16[1024,768]{1,0:T(8,128)(2,1)} %w_hbm.1, bf16[1024,768]{1,0:T(8,128)(2,1)} %m_hbm.1, bf16[512,1024]{1,0:T(8,128)(2,1)} %t_hbm.1), custom_call_target="tpu_custom_call" | custom-call | flops 2415919104 | bytes 6291456 | tf_op jit(solution)/shard_map/pallas_call | solution.py:317
  27.0 1.7 %shard_map.68 = (bf16[1024,768]{1,0:T(8,128)(2,1)}, bf16[1024,768]{1,0:T(8,128)(2,1)}, bf16[96,128]{1,0:T(8,128)(2,1)}) custom-call(bf16[1024,768]{1,0:T(8,128)(2,1)S(1)} %get-tuple-element.9.w_ref, bf16[1024,768]{1,0:T(8,128)(2,1)S(1)} %get-tuple-element.10.m_ref, bf16[96,128]{1,0:T(8,128)(2,1)S(1)} %get-tuple-element.11.g_ref), custom_call_target="tpu_custom_call" | custom-call | tf_op jit(solution)/shard_map/pallas_call | solution.py:356

commit v5 on v4

--- a/solution.py
+++ b/solution.py
@@ -15,6 +15,20 @@
 
 def mult(value, by):
     return value if isinstance(value, int) else pl.multiple_of(value, by)
+
+
+def others(me, count):
+    if count & (count - 1):
+        return [lax.rem(me + d, count) for d in range(1, count)]
+    found = []
+    for mask in range(count - 1, 0, -1):
+        other, bit = 0, 1
+        while bit < count:
+            mine = lax.rem(lax.div(me, bit), 2)
+            other = other + bit * (1 - mine if mask & bit else mine)
+            bit *= 2
+        found.append(other)
+    return found
 
 
 def kernel(
@@ -97,8 +111,7 @@
     def spread(source):
         here = feat_at(source, mine, piece)
         remote(here, here, zs.at[source], zr.at[source], (wide, source)).wait_recv()
-        for d in range(1, split):
-            other = lax.rem(slot + d, split)
+        for other in others(slot, split):
             copy = remote(
                 here, here, ps.at[source, other], pr.at[source, slot],
                 ((group + other) * 2 + core, blk),
@@ -110,8 +123,7 @@
         if source is mate:
             whole = feat_at(source, core * half, half)
             remote(whole, whole, zs.at[source], zr.at[source], (wide, source)).wait_recv()
-        for d in range(1, 1 if source is mate else split):
-            other = lax.rem(slot + d, split)
+        for other in [] if source is mate else others(slot, split):
             there = feat_at(source, core * half + other * piece, piece)
             remote(
                 there, there, ps.at[source, other], pr.at[source, other],
@@ -143,15 +155,18 @@
         tt[p] = t_v[pl.ds(first, 2 * rows), :].T
 
     tiles = width // 128
+    order = list(range(1, pairs)) + [0]
     loads[1].wait()
     turn_weights(0, tiles // 3)
     for source in sources[1:]:
         spread(source)
     turn_weights(tiles // 3, tiles // 2)
+    loads[2].wait()
+    turn_targets(order[0])
     cross(mate)
-    loads[2].wait()
-    turn_targets(0)
     turn_weights(tiles // 2, tiles)
+    for source in sources[1:]:
+        cross(source)
     loads[0].wait()
 
     step = min(512, labels)
@@ -199,8 +214,7 @@
             part[p * 2 + n] = total
             b_send[p * 2 + n] = total.astype(BF16)
         for q in blocks_of(i):
-            for d in range(1, chips):
-                other = lax.rem(chip + d, chips)
+            for other in others(chip, chips):
                 copy = remote(
                     b_send.at[q, other], b_recv.at[q, chip], bs.at[q, other], br.at[q, chip],
                     (other * 2 + core, blk),
@@ -210,8 +224,7 @@
 
     def block_sum(q):
         total = part[q, chip]
-        for d in range(1, chips):
-            other = lax.rem(chip + d, chips)
+        for other in others(chip, chips):
             remote(
                 b_send.at[q, other], b_recv.at[q, other], bs.at[q, other], br.at[q, other],
                 (other * 2 + core, blk),
@@ -245,30 +258,25 @@
             update(n)
         del updates[:count]
 
-    arrived(sources[0])
-    errors(0)
-    for source in sources[1:]:
-        cross(source)
-    first_half(0)
-    second_half(0)
-    for i in range(1, pairs):
-        turn_targets(i)
-    for i in range(1, pairs):
-        arrived(sources[2 * i - 1])
-        arrived(sources[2 * i])
-        to_chips(i - 1)
+    for at, i in enumerate(order):
+        for source in [mate] if i == 0 else sources[2 * i - 1:2 * i + 1]:
+            arrived(source)
+        if at >= 1:
+            to_chips(order[at - 1])
         errors(i)
         first_half(i)
         second_half(i)
-        if i >= 2:
-            to_blocks(i - 2)
-    to_chips(pairs - 1)
+        if at >= 2:
+            to_blocks(order[at - 2])
+        if at + 1 < pairs:
+            turn_targets(order[at + 1])
+    to_chips(order[-1])
     loads[3].wait()
     some_updates(1)
     if pairs >= 2:
-        to_blocks(pairs - 2)
+        to_blocks(order[-2])
     some_updates(2)
-    to_blocks(pairs - 1)
+    to_blocks(order[-1])
     some_updates(len(updates))
 
     total = block_sum(blk)

time: 28.9 us -> 28.4 us (0.983)
  Pallas kernels: 28.1 us -> 27.6 us
    pallas_call x1, Pallas kernels: 26.4 us -> 25.9 us  [shards(): pl.pallas_call(functools.partial(kernel, nw, nb, split), out_shape=(pltpu...]
where the time goes in v5:
time: 28.4 us; the launch traced here: 28.3 us
  Pallas kernels  27.6 us (97%)
  between operations  0.64 us (2%)
    pallas_call x1, Pallas kernels, shards(): pl.pallas_call(functools.partial(kernel, nw, nb, split), out_shape=(pltpu...  25.9 us
    pallas_call x1, Pallas kernels, shards(): pl.pallas_call(keep, out_shape=tuple((jax.ShapeDtypeStruct(shape, BF16) f...  1.74 us

profile of v5, /device:TPU:0, one launch (start us, length us, event | category | flops | bytes accessed | tf_op | source)
XLA Modules:
  0.0 28.3 jit_solution(12555978718224358774)
XLA Ops:
  0.6 25.9 %shard_map.67 = (bf16[1024,768]{1,0:T(8,128)(2,1)S(1)}, bf16[1024,768]{1,0:T(8,128)(2,1)S(1)}, bf16[96,128]{1,0:T(8,128)(2,1)S(1)}) custom-call(bf16[128,768]{1,0:T(8,128)(2,1)} %feat_ref.1, bf16[1024,768]{1,0:T(8,128)(2,1)} %w_hbm.1, bf16[1024,768]{1,0:T(8,128)(2,1)} %m_hbm.1, bf16[512,1024]{1,0:T(8,128)(2,1)} %t_hbm.1), custom_call_target="tpu_custom_call" | custom-call | flops 2415919104 | bytes 6291456 | tf_op jit(solution)/shard_map/pallas_call | solution.py:325
  26.5 1.7 %shard_map.68 = (bf16[1024,768]{1,0:T(8,128)(2,1)}, bf16[1024,768]{1,0:T(8,128)(2,1)}, bf16[96,128]{1,0:T(8,128)(2,1)}) custom-call(bf16[1024,768]{1,0:T(8,128)(2,1)S(1)} %get-tuple-element.9.w_ref, bf16[1024,768]{1,0:T(8,128)(2,1)S(1)} %get-tuple-element.10.m_ref, bf16[96,128]{1,0:T(8,128)(2,1)S(1)} %get-tuple-element.11.g_ref), custom_call_target="tpu_custom_call" | custom-call | tf_op jit(solution)/shard_map/pallas_call | solution.py:364

commit v6 on v5

--- a/solution.py
+++ b/solution.py
@@ -271,11 +271,10 @@
         if at + 1 < pairs:
             turn_targets(order[at + 1])
     to_chips(order[-1])
-    loads[3].wait()
-    some_updates(1)
     if pairs >= 2:
         to_blocks(order[-2])
-    some_updates(2)
+    loads[3].wait()
+    some_updates(3)
     to_blocks(order[-1])
     some_updates(len(updates))
 

time: 28.4 us -> 28.3 us (level)
  no operation moved by 1% of the time
where the time goes in v6:
time: 28.3 us; the launch traced here: 28.1 us
  Pallas kernels  27.5 us (97%)
  between operations  0.64 us (2%)
    pallas_call x1, Pallas kernels, shards(): pl.pallas_call(functools.partial(kernel, nw, nb, split), out_shape=(pltpu...  25.8 us
    pallas_call x1, Pallas kernels, shards(): pl.pallas_call(keep, out_shape=tuple((jax.ShapeDtypeStruct(shape, BF16) f...  1.74 us

profile of v6, /device:TPU:0, one launch (start us, length us, event | category | flops | bytes accessed | tf_op | source)
XLA Modules:
  0.0 28.1 jit_solution(184436652816482359)
XLA Ops:
  0.6 25.8 %shard_map.67 = (bf16[1024,768]{1,0:T(8,128)(2,1)S(1)}, bf16[1024,768]{1,0:T(8,128)(2,1)S(1)}, bf16[96,128]{1,0:T(8,128)(2,1)S(1)}) custom-call(bf16[128,768]{1,0:T(8,128)(2,1)} %feat_ref.1, bf16[1024,768]{1,0:T(8,128)(2,1)} %w_hbm.1, bf16[1024,768]{1,0:T(8,128)(2,1)} %m_hbm.1, bf16[512,1024]{1,0:T(8,128)(2,1)} %t_hbm.1), custom_call_target="tpu_custom_call" | custom-call | flops 2415919104 | bytes 6291456 | tf_op jit(solution)/shard_map/pallas_call | solution.py:324
  26.4 1.7 %shard_map.68 = (bf16[1024,768]{1,0:T(8,128)(2,1)}, bf16[1024,768]{1,0:T(8,128)(2,1)}, bf16[96,128]{1,0:T(8,128)(2,1)}) custom-call(bf16[1024,768]{1,0:T(8,128)(2,1)S(1)} %get-tuple-element.9.w_ref, bf16[1024,768]{1,0:T(8,128)(2,1)S(1)} %get-tuple-element.10.m_ref, bf16[96,128]{1,0:T(8,128)(2,1)S(1)} %get-tuple-element.11.g_ref), custom_call_target="tpu_custom_call" | custom-call | tf_op jit(solution)/shard_map/pallas_call | solution.py:363
